TPU v7x, 512 devices: a whole 4x4x16 slice. The times are simulated.
512 devices in a mesh: clip: 32 (over x_hi, z), frame: 16 (over y, x_lo, core).
Axes of the slice: x: 4 (x_hi: 2, x_lo: 2; x = x_hi * 2 + x_lo), y: 4, z: 16, core: 2. Of those that a mesh axis runs over, the one named last changes fastest.
Arguments:
- clips: bfloat16 [32, 16, 16, 32, 256], P('clip', 'frame'), may hold values from -25 to 25, as said below
- cotangent: bfloat16 [32, 16, 16, 32, 256], P('clip', 'frame'), may hold values from -25 to 25
- norm_gain: float32 [256], replicated, may hold values from 0.25 to 1.75
- norm_shift: float32 [256], replicated, may hold values from -3 to 3
- w_spatial: bfloat16 [3, 3, 256, 256], replicated, may hold values from -0.125 to 0.125
- w_time: bfloat16 [3, 256, 256], replicated, may hold values from -0.21875 to 0.21875
Outputs:
- result_video: bfloat16 [32, 16, 16, 32, 256], P('clip', 'frame')
- input_grad: bfloat16 [32, 16, 16, 32, 256], P('clip', 'frame')
- spatial_grad: bfloat16 [3, 3, 256, 256], P(None, None, 'frame')
- time_grad: bfloat16 [3, 256, 256], P(None, 'frame')
Inputs may be any that keep to these rules, and one draw needn't show every extreme that they name: `clips`: input activations.
All inputs are finite; a program needn't handle non-finite values.
Results may differ from a plain program's by a relative error of at most 0.0029.
Values may be sent and summed in bfloat16 or wider, within the bound.
A program may use at most 64 MiB of HBM per device.

v0:
```python
import math
import jax
import jax.numpy as jnp
from jax import lax
from jax.sharding import PartitionSpec as P

GROUPS = 32
epsilon = 1e-05


def group_sums(values, groups):
    return values.reshape(groups, -1).sum(axis=1)


def spread_groups(values, channels):
    return jnp.repeat(values, channels // values.shape[0])


def spatial_conv(hidden, weights):
    row_count, col_count, channels = (hidden.shape[1], hidden.shape[2], hidden.shape[3])
    padded = jnp.pad(hidden, ((0, 0), (1, 1), (1, 1), (0, 0)))
    running = jnp.zeros((hidden.shape[0] * row_count * col_count, weights.shape[-1]), jnp.float32)
    for row_tap in range(3):
        for col_tap in range(3):
            window = padded[
                :, row_tap : row_tap + row_count, col_tap : col_tap + col_count, :
            ].reshape(-1, channels)
            running = running + jnp.dot(
                window, weights[row_tap, col_tap], preferred_element_type=jnp.float32
            )
    return running.reshape(hidden.shape[:-1] + (weights.shape[-1],))


def spatial_weights(hidden, gradient):
    row_count, col_count, channels = (hidden.shape[1], hidden.shape[2], hidden.shape[3])
    padded = jnp.pad(hidden, ((0, 0), (1, 1), (1, 1), (0, 0)))
    flat_grad = gradient.reshape(-1, gradient.shape[-1])
    rows_out = []
    for row_tap in range(3):
        cols_out = []
        for col_tap in range(3):
            window = padded[
                :, row_tap : row_tap + row_count, col_tap : col_tap + col_count, :
            ].reshape(-1, channels)
            cols_out.append(jnp.dot(window.T, flat_grad, preferred_element_type=jnp.float32))
        rows_out.append(jnp.stack(cols_out))
    return jnp.stack(rows_out)


def causal_conv(sequence, w_time):
    frames, channels = (sequence.shape[0], sequence.shape[-1])
    padded = jnp.pad(sequence, ((2, 0),) + ((0, 0),) * (sequence.ndim - 1))
    running = jnp.zeros((sequence.size // channels, channels), jnp.float32)
    for offset in range(3):
        running = running + jnp.dot(
            padded[2 - offset : 2 - offset + frames].reshape(-1, channels),
            w_time[offset],
            preferred_element_type=jnp.float32,
        )
    return running.reshape(sequence.shape)


def causal_back(gradient, w_time):
    frames, channels = (gradient.shape[0], gradient.shape[-1])
    padded = jnp.pad(gradient, ((0, 2),) + ((0, 0),) * (gradient.ndim - 1))
    running = jnp.zeros((gradient.size // channels, channels), jnp.float32)
    for offset in range(3):
        running = running + jnp.dot(
            padded[offset : offset + frames].reshape(-1, channels),
            w_time[offset].T,
            preferred_element_type=jnp.float32,
        )
    return running.reshape(gradient.shape)


def causal_weights(sequence, gradient):
    frames, channels = (sequence.shape[0], sequence.shape[-1])
    padded = jnp.pad(sequence, ((2, 0),) + ((0, 0),) * (sequence.ndim - 1))
    flat_grad = gradient.reshape(-1, channels)
    return jnp.stack(
        [
            jnp.dot(
                padded[2 - offset : 2 - offset + frames].reshape(-1, channels).T,
                flat_grad,
                preferred_element_type=jnp.float32,
            )
            for offset in range(3)
        ]
    )


def per_device(clips, cotangent, norm_gain, norm_shift, w_spatial, w_time):
    frame_count = lax.axis_size("frame")
    clip_count = lax.axis_size("clip")
    video_frame = clips[0]
    grad_frame = cotangent[0]
    row_count, col_count, channels = (
        video_frame.shape[1],
        video_frame.shape[2],
        video_frame.shape[3],
    )
    members = frame_count * row_count * col_count * (channels // GROUPS)
    values = video_frame.astype(jnp.float32)
    value_sum = lax.psum(group_sums(jnp.sum(values, axis=(0, 1, 2)), GROUPS), "frame")
    center = value_sum / members
    centered = values - spread_groups(center, channels)
    square_sum = lax.psum(group_sums(jnp.sum(centered * centered, axis=(0, 1, 2)), GROUPS), "frame")
    variance = square_sum / members
    inv_std = lax.rsqrt(variance + epsilon)
    normed = centered * spread_groups(inv_std, channels)
    activation = normed * norm_gain + norm_shift
    hidden = jax.nn.silu(activation).astype(jnp.bfloat16)
    mixed_frame = spatial_conv(hidden, w_spatial).astype(jnp.bfloat16)
    mixed_band, grad_band = (
        lax.all_to_all(mixed_frame[None], "frame", split_axis=2, concat_axis=1, tiled=True),
        lax.all_to_all(cotangent, "frame", split_axis=2, concat_axis=1, tiled=True),
    )
    band_out = causal_conv(mixed_band[0], w_time).astype(jnp.bfloat16)
    back_band = causal_back(grad_band[0], w_time).astype(jnp.bfloat16)
    time_part = causal_weights(mixed_band[0], grad_band[0])
    temporal, mixed_home = (
        lax.all_to_all(band_out[None], "frame", split_axis=1, concat_axis=2, tiled=True),
        lax.all_to_all(back_band[None], "frame", split_axis=1, concat_axis=2, tiled=True),
    )
    mixed_grad = mixed_home[0]
    result_video = (clips.astype(jnp.float32) + temporal.astype(jnp.float32)).astype(jnp.bfloat16)
    spatial_part = spatial_weights(hidden, mixed_grad)
    flipped = jnp.swapaxes(w_spatial[::-1, ::-1], 2, 3)
    hidden_grad = spatial_conv(mixed_grad, flipped)
    sigmoid_act = jax.nn.sigmoid(activation)
    act_grad = hidden_grad * sigmoid_act * (1.0 + activation * (1.0 - sigmoid_act))
    normed_grad = act_grad * norm_gain
    first_sum, second_sum = lax.psum(
        (
            group_sums(jnp.sum(normed_grad, axis=(0, 1, 2)), GROUPS),
            group_sums(jnp.sum(normed_grad * normed, axis=(0, 1, 2)), GROUPS),
        ),
        "frame",
    )
    input_grad = grad_frame.astype(jnp.float32) + spread_groups(inv_std, channels) * (
        normed_grad
        - spread_groups(first_sum / members, channels)
        - normed * spread_groups(second_sum / members, channels)
    )
    stacked = jnp.concatenate([spatial_part.reshape(9, channels, channels), time_part], axis=0)
    grad_share = lax.psum_scatter(stacked, "frame", scatter_dimension=1, tiled=True)
    grad_share = lax.psum(grad_share, "clip")
    grad_scale = 1.0 / math.sqrt(clip_count * frame_count * row_count * col_count)
    grad_share = grad_share * grad_scale
    spatial_out = grad_share[:9].reshape(3, 3, grad_share.shape[1], channels).astype(jnp.bfloat16)
    time_out = grad_share[9:].astype(jnp.bfloat16)
    return (result_video, input_grad.astype(jnp.bfloat16)[None], spatial_out, time_out)


def solution(mesh):
    placed = (
        P("clip", "frame", None, None, None),
        P("clip", "frame", None, None, None),
        P(),
        P(),
        P(),
        P(),
    )
    return jax.shard_map(
        per_device,
        mesh=mesh,
        in_specs=placed,
        out_specs=(
            P("clip", "frame", None, None, None),
            P("clip", "frame", None, None, None),
            P(None, None, "frame", None),
            P(None, "frame", None),
        ),
        check_vma=False,
    )
```

profile of v0, /device:TPU:8, one launch (start us, length us, event | category | flops | bytes accessed | tf_op | source)
XLA Modules:
  0.0 527.7 jit_solution(11038506905976836317)
XLA Ops:
  7.2 9.3 %all-to-all-start.2 = ((bf16[1,1,16,32,256]{4,3,1,0,2:T(8,128)(2,1)}), bf16[1,1,16,32,256]{4,3,1,0,2:T(8,128)(2,1)S(1)}, u32[]{:S(2)}, u32[]{:S(2)}) async-start(bf16[1,1,16,32,256]{4,3,1,0,2:T(8,128)(2,1)} %bitcast.264), calls=%async_computation.2 | async-start | bytes 524288 | tf_op jit(solution)/shard_map/all_to_all | solution.py:116
  16.5 1.0 convert_reduce_fusion
  17.7 23.8 %psum.35 = f32[32]{0:T(128)S(1)} all-reduce(f32[32]{0:T(128)S(1)} %reduce_sum.73), channel_id=1, replica_groups=mesh['clip'=32,'frame'=16] {'frame'}, use_global_device_ids=true, to_apply=%region_2.0 | all-reduce | flops 32 | bytes 256 | tf_op jit(solution)/shard_map/psum | solution.py:104
  41.7 1.1 multiply_reduce_fusion.1
  43.0 27.1 %psum.36 = f32[32]{0:T(128)S(1)} all-reduce(f32[32]{0:T(128)S(1)} %reduce_sum.75), channel_id=1, replica_groups=mesh['clip'=32,'frame'=16] {'frame'}, use_global_device_ids=true, to_apply=%region_5.0 | all-reduce | flops 32 | bytes 256 | tf_op jit(solution)/shard_map/psum | solution.py:107
  70.6 1.0 pad_slice_fusion.8
  71.5 0.4 copy-done.1
  71.9 1.2 reverse_bitcast_fusion
  73.6 1.1 convolution_add_fusion.18
  74.7 1.2 fusion.12
  76.2 1.0 fusion.2
  77.2 10.6 %all-to-all-start.3 = ((bf16[1,16,1,32,256]{4,3,2,0,1:T(8,128)(2,1)}), bf16[1,16,1,32,256]{4,3,2,0,1:T(8,128)(2,1)S(1)}, u32[]{:S(2)}, u32[]{:S(2)}) async-start(bf16[1,16,1,32,256]{4,3,2,0,1:T(8,128)(2,1)} %bitcast.266), calls=%async_computation.3 | async-start | bytes 524288 | tf_op jit(solution)/shard_map/all_to_all | solution.py:123
  87.8 2.2 convolution_add_fusion.17
  90.0 3.3 all-to-all-done.3
  93.3 1.9 convolution_bitcast_fusion.8
  95.2 1.9 convolution_bitcast_fusion.9
  97.2 1.9 convolution_bitcast_fusion.10
  99.1 1.0 convolution_bitcast_fusion.11
  100.0 0.3 pad_slice_fusion
  100.3 1.0 copy-done.2
  102.1 0.3 convolution_add_fusion.5
  102.6 0.3 convolution_add_fusion.3
  103.2 0.3 convolution_add_fusion.1
  103.4 1.2 fusion.41
  105.1 24.8 %all-reduce.4 = (f32[32]{0:T(128)S(1)}, f32[32]{0:T(128)S(1)}) all-reduce(f32[32]{0:T(128)S(1)} %reduce_sum.79, f32[32]{0:T(128)S(1)} %reduce_sum.77), channel_id=1, replica_groups=mesh['clip'=32,'frame'=16] {'frame'}, use_global_device_ids=true, to_apply=%region_11.12 | all-reduce | flops 64 | bytes 512 | tf_op jit(solution)/shard_map/psum | solution.py:133
  130.2 2.3 add_convert_fusion
  132.5 1.0 convolution_bitcast_fusion.7
  133.7 0.3 convolution_bitcast_fusion.6
  134.2 0.3 convolution_bitcast_fusion.5
  134.7 1.0 convolution_bitcast_fusion.4
  135.9 1.0 convolution_bitcast_fusion.3
  136.9 0.9 fusion
  137.8 9.2 %all-to-all-start = ((bf16[1,1,16,32,256]{4,3,1,0,2:T(8,128)(2,1)}), bf16[1,1,16,32,256]{4,3,1,0,2:T(8,128)(2,1)S(1)}, u32[]{:S(2)}, u32[]{:S(2)}) async-start(bf16[1,1,16,32,256]{4,3,1,0,2:T(8,128)(2,1)} %bitcast.265), calls=%async_computation | async-start | bytes 524288 | tf_op jit(solution)/shard_map/all_to_all | solution.py:115
  147.0 1.0 maximum_bitcast_fusion.2
  148.1 0.9 copy-done.10
  149.4 3.1 all-to-all-done
  152.8 0.3 convolution_bitcast_fusion.1
  153.1 0.3 convolution_bitcast_fusion.2
  153.4 2.0 pad_maximum_fusion
  155.4 1.0 copy-done.9
  156.9 0.9 fusion.1
  157.8 6.0 %all-to-all-start.1 = ((bf16[1,16,1,32,256]{4,3,2,0,1:T(8,128)(2,1)}), bf16[1,16,1,32,256]{4,3,2,0,1:T(8,128)(2,1)S(1)}, u32[]{:S(2)}, u32[]{:S(2)}) async-start(bf16[1,16,1,32,256]{4,3,2,0,1:T(8,128)(2,1)} %bitcast.29), calls=%async_computation.1 | async-start | bytes 524288 | tf_op jit(solution)/shard_map/all_to_all | solution.py:122
  163.9 59.5 %reduce-scatter.2.cloned.1.call-done = f32[12,16,256]{2,1,0:T(8,128)} async-done(((f32[12,256,256]{2,1,0:T(8,128)}), f32[12,16,256]{2,1,0:T(8,128)}) %reduce-scatter.2.cloned.1.call-update) | async-done | bytes 196624 | tf_op jit(solution)/shard_map/reduce_scatter | solution.py:146
  223.5 0.8 fusion.3
  224.3 294.4 %all-reduce.7.cloned.1.call-done = f32[12,16,256]{2,1,0:T(8,128)} async-done(((f32[12,16,256]{2,1,0:T(8,128)}), f32[12,16,256]{2,1,0:T(8,128)}) %all-reduce.7.cloned.1.call-update) | async-done | bytes 196624 | tf_op jit(solution)/shard_map/psum | solution.py:147
  518.6 0.9 multiply_convert_fusion.2
  519.6 0.6 slice.202
  520.2 0.6 slice.203
  (78 shorter events, 6.0 us)
Async XLA Ops:
  7.2 63.2 %copy-start = (bf16[1,1,16,32,256]{4,3,2,1,0:T(8,128)(2,1)S(1)}, bf16[1,1,16,32,256]{4,3,2,1,0:T(8,128)(2,1)}, u32[]{:S(2)}) copy-start(bf16[1,1,16,32,256]{4,3,2,1,0:T(8,128)(2,1)} %param.6) | copy-start | bytes 786436
  7.2 63.1 %copy-start.16 = (f32[256]{0:T(256)S(1)}, f32[256]{0:T(256)}, u32[]{:S(2)}) copy-start(f32[256]{0:T(256)} %param.9) | copy-start | bytes 3076
  7.2 63.1 %copy-start.17 = (f32[256]{0:T(256)S(1)}, f32[256]{0:T(256)}, u32[]{:S(2)}) copy-start(f32[256]{0:T(256)} %param.8) | copy-start | bytes 3076
  7.2 67.5 %all-to-all-start.2 = ((bf16[1,1,16,32,256]{4,3,1,0,2:T(8,128)(2,1)}), bf16[1,1,16,32,256]{4,3,1,0,2:T(8,128)(2,1)S(1)}, u32[]{:S(2)}, u32[]{:S(2)}) async-start(bf16[1,1,16,32,256]{4,3,1,0,2:T(8,128)(2,1)} %bitcast.264), calls=%async_computation.2 | async-start | bytes 524288 | tf_op jit(solution)/shard_map/all_to_all | solution.py:116
  70.5 1.4 copy-start.1
  71.9 1.7 copy-start.3
  71.9 1.7 copy-start.4
  74.7 1.3 copy-start.8
  77.2 16.1 %all-to-all-start.3 = ((bf16[1,16,1,32,256]{4,3,2,0,1:T(8,128)(2,1)}), bf16[1,16,1,32,256]{4,3,2,0,1:T(8,128)(2,1)S(1)}, u32[]{:S(2)}, u32[]{:S(2)}) async-start(bf16[1,16,1,32,256]{4,3,2,0,1:T(8,128)(2,1)} %bitcast.266), calls=%async_computation.3 | async-start | bytes 524288 | tf_op jit(solution)/shard_map/all_to_all | solution.py:123
  100.0 1.3 copy-start.2
  130.2 3.2 copy-start.7
  135.9 11.1 %copy-start.15 = (f32[1,256,256]{2,1,0:T(8,128)S(1)}, f32[1,256,256]{2,1,0:T(8,128)}, u32[]{:S(2)}) copy-start(f32[1,256,256]{2,1,0:T(8,128)} %convolution_bitcast_fusion.4) | copy-start | bytes 786436
  137.8 10.2 %copy-start.12 = (f32[1,256,256]{2,1,0:T(8,128)S(1)}, f32[1,256,256]{2,1,0:T(8,128)}, u32[]{:S(2)}) copy-start(f32[1,256,256]{2,1,0:T(8,128)} %convolution_bitcast_fusion.8) | copy-start | bytes 786436
  137.8 10.3 %copy-start.14 = (f32[1,256,256]{2,1,0:T(8,128)S(1)}, f32[1,256,256]{2,1,0:T(8,128)}, u32[]{:S(2)}) copy-start(f32[1,256,256]{2,1,0:T(8,128)} %convolution_bitcast_fusion.7) | copy-start | bytes 786436
  137.8 14.7 %all-to-all-start = ((bf16[1,1,16,32,256]{4,3,1,0,2:T(8,128)(2,1)}), bf16[1,1,16,32,256]{4,3,1,0,2:T(8,128)(2,1)S(1)}, u32[]{:S(2)}, u32[]{:S(2)}) async-start(bf16[1,1,16,32,256]{4,3,1,0,2:T(8,128)(2,1)} %bitcast.265), calls=%async_computation | async-start | bytes 524288 | tf_op jit(solution)/shard_map/all_to_all | solution.py:115
  147.0 76.5 %reduce-scatter.2.cloned.1.call-start = ((), (), s32[]{:S(2)}) async-start(), calls=%async_computation.5 | async-start | bytes 3342336 | tf_op jit(solution)/shard_map/reduce_scatter | solution.py:146
  148.0 1.0 copy-start.10
  148.1 1.0 copy-start.11
  148.1 1.1 copy-start.13
  152.5 0.8 copy-start.5
  155.4 1.0 copy-start.9
  155.4 1.2 copy-start.6
  157.8 65.7 %all-to-all-start.1 = ((bf16[1,16,1,32,256]{4,3,2,0,1:T(8,128)(2,1)}), bf16[1,16,1,32,256]{4,3,2,0,1:T(8,128)(2,1)S(1)}, u32[]{:S(2)}, u32[]{:S(2)}) async-start(bf16[1,16,1,32,256]{4,3,2,0,1:T(8,128)(2,1)} %bitcast.29), calls=%async_computation.1 | async-start | bytes 524288 | tf_op jit(solution)/shard_map/all_to_all | solution.py:122
  163.8 354.8 %all-reduce.7.cloned.1.call-start = ((), (), s32[]{:S(2)}) async-start(), calls=%async_computation.6 | async-start | bytes 393216 | tf_op jit(solution)/shard_map/psum | solution.py:147
Sparse Core Ops, SparseCore 0:
  155.6 67.8 reduce-scatter.1
  226.3 292.2 all-reduce.6
where the time goes:
time: 529 us; the launch traced here: 528 us
  waiting for transfers between devices  360 us (68%)
  blocking collectives  75.7 us (14%)
  starting transfers between devices  35.2 us (7%)
  matrix products  23.5 us (4%)
  between operations  14.5 us (3%)
  other arithmetic  10.1 us (2%)
  local copies, waits for them, and re-layouts  8.18 us (2%)
    psum x1, waiting for transfers between devices, per_device(): grad_share = lax.psum(grad_share, 'clip')  294 us
    reduce_scatter x1, waiting for transfers between devices, per_device(): lax.psum_scatter(stacked, 'frame', scatter_dimension=1, tiled=True)  59.5 us
    psum x1, blocking collectives, per_device(): lax.psum(group_sums(jnp.sum(centered * centered, axis=(0, 1, 2)), GROUPS)...  27.1 us
    psum x1, blocking collectives, per_device(): lax.psum((group_sums(jnp.sum(normed_grad, axis=(0, 1, 2)), GROUPS), group...  24.8 us
    psum x1, blocking collectives, per_device(): lax.psum(group_sums(jnp.sum(values, axis=(0, 1, 2)), GROUPS), 'frame')  23.8 us
    all_to_all x1, starting transfers between devices, per_device(): lax.all_to_all(back_band[None], 'frame', split_axis=1, concat_axis=2, til...  10.6 us
  transfers between devices with their start and end apart: 6, of which 4 were waited for; matrix products, arithmetic and copies ran while one was open for 2% of the time, Pallas kernels for 0%

commit v1 on v0

--- a/solution.py
+++ b/solution.py
@@ -144,7 +144,7 @@
     )
     stacked = jnp.concatenate([spatial_part.reshape(9, channels, channels), time_part], axis=0)
     grad_share = lax.psum_scatter(stacked, "frame", scatter_dimension=1, tiled=True)
-    grad_share = lax.psum(grad_share, "clip")
+    grad_share = jnp.sum(lax.all_gather(grad_share, "clip"), axis=0)
     grad_scale = 1.0 / math.sqrt(clip_count * frame_count * row_count * col_count)
     grad_share = grad_share * grad_scale
     spatial_out = grad_share[:9].reshape(3, 3, grad_share.shape[1], channels).astype(jnp.bfloat16)

time: 529 us -> 421 us (0.80)
  the two profiles are of different devices: /device:TPU:8 before, /device:TPU:32 now
where the time goes in v1:
time: 421 us; the launch traced here: 420 us
  waiting for transfers between devices  257 us (61%)
  blocking collectives  96.5 us (23%)
  matrix products  20.6 us (5%)
  between operations  14.6 us (3%)
  starting transfers between devices  12.9 us (3%)
  other arithmetic  12.5 us (3%)
  local copies, waits for them, and re-layouts  6.79 us (2%)
    all_gather x1, waiting for transfers between devices, per_device(): grad_share = jnp.sum(lax.all_gather(grad_share, 'clip'), axis=0)  169 us
    reduce_scatter x1, waiting for transfers between devices, per_device(): lax.psum_scatter(stacked, 'frame', scatter_dimension=1, tiled=True)  76.1 us
    psum x1, blocking collectives, per_device(): lax.psum(group_sums(jnp.sum(values, axis=(0, 1, 2)), GROUPS), 'frame')  30.9 us
    psum x1, blocking collectives, per_device(): lax.psum((group_sums(jnp.sum(normed_grad, axis=(0, 1, 2)), GROUPS), group...  27.8 us
    psum x1, blocking collectives, per_device(): lax.psum(group_sums(jnp.sum(centered * centered, axis=(0, 1, 2)), GROUPS)...  27.1 us
    all_to_all x1, blocking collectives, per_device(): lax.all_to_all(band_out[None], 'frame', split_axis=1, concat_axis=2, tile...  10.6 us
    dot_general x18, matrix products, spatial_conv(): jnp.dot(window, weights[row_tap, col_tap], preferred_element_type=jnp.flo...  8.82 us
  transfers between devices with their start and end apart: 5, of which 4 were waited for; matrix products, arithmetic and copies ran while one was open for 3% of the time, Pallas kernels for 0%

profile of v1, /device:TPU:32, one launch (start us, length us, event | category | flops | bytes accessed | tf_op | source)
XLA Modules:
  0.0 420.4 jit_solution(5305713201452121018)
XLA Ops:
  7.2 5.6 %all-to-all-start.2 = ((bf16[1,1,16,32,256]{4,3,1,0,2:T(8,128)(2,1)}), bf16[1,1,16,32,256]{4,3,1,0,2:T(8,128)(2,1)S(1)}, u32[]{:S(2)}, u32[]{:S(2)}) async-start(bf16[1,1,16,32,256]{4,3,1,0,2:T(8,128)(2,1)} %bitcast.266), calls=%async_computation.2 | async-start | bytes 524288 | tf_op jit(solution)/shard_map/all_to_all | solution.py:116
  12.9 1.0 convert_reduce_fusion
  14.1 30.9 %psum.28 = f32[32]{0:T(128)S(1)} all-reduce(f32[32]{0:T(128)S(1)} %reduce_sum.82), channel_id=1, replica_groups=mesh['clip'=32,'frame'=16] {'frame'}, use_global_device_ids=true, to_apply=%region_2.0 | all-reduce | flops 32 | bytes 256 | tf_op jit(solution)/shard_map/psum | solution.py:104
  45.2 1.1 multiply_reduce_fusion.1
  46.5 27.1 %psum.29 = f32[32]{0:T(128)S(1)} all-reduce(f32[32]{0:T(128)S(1)} %reduce_sum.84), channel_id=1, replica_groups=mesh['clip'=32,'frame'=16] {'frame'}, use_global_device_ids=true, to_apply=%region_5.0 | all-reduce | flops 32 | bytes 256 | tf_op jit(solution)/shard_map/psum | solution.py:107
  74.0 1.2 pad_slice_fusion.8
  75.3 0.5 copy-done.1
  76.1 0.4 copy-done.6
  76.7 1.0 convolution_add_fusion.18
  77.8 1.2 fusion.12
  79.3 1.0 fusion.2
  80.2 3.5 all-to-all-start.3
  83.8 2.2 convolution_add_fusion.17
  85.9 5.9 %all-to-all-done.3 = bf16[1,16,1,32,256]{4,3,2,0,1:T(8,128)(2,1)S(1)} async-done(((bf16[1,16,1,32,256]{4,3,2,0,1:T(8,128)(2,1)}), bf16[1,16,1,32,256]{4,3,2,0,1:T(8,128)(2,1)S(1)}, u32[]{:S(2)}, u32[]{:S(2)}) %all-to-all-start.3) | async-done | bytes 262176 | tf_op jit(solution)/shard_map/all_to_all | solution.py:123
  91.8 2.0 convolution_bitcast_fusion.8
  93.7 1.9 convolution_bitcast_fusion.9
  95.7 1.0 convolution_bitcast_fusion.10
  96.7 1.0 convolution_bitcast_fusion.11
  97.6 0.3 pad_slice_fusion
  99.3 0.3 convolution_add_fusion.3
  99.5 0.3 convolution_add_fusion.2
  99.8 0.3 convolution_add_fusion.1
  100.1 1.3 fusion.41
  101.8 27.8 %all-reduce.4 = (f32[32]{0:T(128)S(1)}, f32[32]{0:T(128)S(1)}) all-reduce(f32[32]{0:T(128)S(1)} %reduce_sum.88, f32[32]{0:T(128)S(1)} %reduce_sum.86), channel_id=1, replica_groups=mesh['clip'=32,'frame'=16] {'frame'}, use_global_device_ids=true, to_apply=%region_11.12 | all-reduce | flops 64 | bytes 512 | tf_op jit(solution)/shard_map/psum | solution.py:133
  129.9 2.2 add_convert_fusion
  132.1 0.3 convolution_bitcast_fusion.7
  132.7 0.4 copy-done.5
  133.1 0.3 convolution_bitcast_fusion.6
  133.6 0.3 convolution_bitcast_fusion.5
  134.1 0.4 copy-done.3
  134.5 0.3 convolution_bitcast_fusion.4
  135.1 1.0 convolution_bitcast_fusion.3
  136.1 0.9 fusion
  137.0 3.7 all-to-all-start
  140.7 1.0 maximum_bitcast_fusion.2
  141.8 0.9 copy-done.14
  143.1 5.6 %all-to-all-done = bf16[1,1,16,32,256]{4,3,1,0,2:T(8,128)(2,1)S(1)} async-done(((bf16[1,1,16,32,256]{4,3,1,0,2:T(8,128)(2,1)}), bf16[1,1,16,32,256]{4,3,1,0,2:T(8,128)(2,1)S(1)}, u32[]{:S(2)}, u32[]{:S(2)}) %all-to-all-start) | async-done | bytes 262176 | tf_op jit(solution)/shard_map/all_to_all | solution.py:115
  148.7 0.3 convolution_bitcast_fusion
  149.0 0.3 convolution_bitcast_fusion.1
  149.3 0.3 convolution_bitcast_fusion.2
  149.6 2.0 pad_maximum_fusion
  151.7 76.1 %reduce-scatter.2.cloned.1.call-done = f32[12,16,256]{2,1,0:T(8,128)} async-done(((f32[12,256,256]{2,1,0:T(8,128)}), f32[12,16,256]{2,1,0:T(8,128)}) %reduce-scatter.2.cloned.1.call-update) | async-done | bytes 196624 | tf_op jit(solution)/shard_map/reduce_scatter | solution.py:146
  228.5 10.6 %all_to_all.16 = bf16[1,16,1,32,256]{4,3,2,0,1:T(8,128)(2,1)S(1)} all-to-all(bf16[1,16,1,32,256]{4,3,2,0,1:T(8,128)(2,1)S(1)} %bitcast.269), channel_id=1, replica_groups=mesh['clip'=32,'frame'=16] {'frame'}, dimensions={1} | all-to-all | bytes 524288 | tf_op jit(solution)/shard_map/all_to_all | solution.py:122
  239.2 0.8 fusion.3
  239.9 169.0 %all-gather.3.cloned.1.call-done = f32[384,16,256]{2,1,0:T(8,128)} async-done(((f32[12,16,256]{2,1,0:T(8,128)}), f32[384,16,256]{2,1,0:T(8,128)}) %all-gather.3.cloned.1.call-update) | async-done | bytes 6291472 | tf_op jit(solution)/shard_map/all_gather | solution.py:147
  408.9 3.4 reduce_sum.89
  412.4 0.6 slice.202
  413.0 0.6 slice.203
  (84 shorter events, 6.1 us)
Async XLA Ops:
  7.2 66.6 %copy-start = (bf16[1,1,16,32,256]{4,3,2,1,0:T(8,128)(2,1)S(1)}, bf16[1,1,16,32,256]{4,3,2,1,0:T(8,128)(2,1)}, u32[]{:S(2)}) copy-start(bf16[1,1,16,32,256]{4,3,2,1,0:T(8,128)(2,1)} %param.6) | copy-start | bytes 786436
  7.2 66.6 %copy-start.19 = (f32[256]{0:T(256)S(1)}, f32[256]{0:T(256)}, u32[]{:S(2)}) copy-start(f32[256]{0:T(256)} %param.9) | copy-start | bytes 3076
  7.2 66.6 %copy-start.20 = (f32[256]{0:T(256)S(1)}, f32[256]{0:T(256)}, u32[]{:S(2)}) copy-start(f32[256]{0:T(256)} %param.8) | copy-start | bytes 3076
  7.2 70.5 %all-to-all-start.2 = ((bf16[1,1,16,32,256]{4,3,1,0,2:T(8,128)(2,1)}), bf16[1,1,16,32,256]{4,3,1,0,2:T(8,128)(2,1)S(1)}, u32[]{:S(2)}, u32[]{:S(2)}) async-start(bf16[1,1,16,32,256]{4,3,1,0,2:T(8,128)(2,1)} %bitcast.266), calls=%async_computation.2 | async-start | bytes 524288 | tf_op jit(solution)/shard_map/all_to_all | solution.py:116
  74.0 1.7 copy-start.1
  75.8 0.7 copy-start.6
  75.8 0.9 copy-start.8
  77.7 1.3 copy-start.12
  80.2 11.6 %all-to-all-start.3 = ((bf16[1,16,1,32,256]{4,3,2,0,1:T(8,128)(2,1)}), bf16[1,16,1,32,256]{4,3,2,0,1:T(8,128)(2,1)S(1)}, u32[]{:S(2)}, u32[]{:S(2)}) async-start(bf16[1,16,1,32,256]{4,3,2,0,1:T(8,128)(2,1)} %bitcast.268), calls=%async_computation.3 | async-start | bytes 524288 | tf_op jit(solution)/shard_map/all_to_all | solution.py:123
  91.8 3.9 copy-start.7
  100.1 29.8 %copy-start.18 = (bf16[1,1,16,32,256]{4,3,2,1,0:T(8,128)(2,1)S(1)}, bf16[1,1,16,32,256]{4,3,2,1,0:T(8,128)(2,1)}, u32[]{:S(2)}) copy-start(bf16[1,1,16,32,256]{4,3,2,1,0:T(8,128)(2,1)} %param.7) | copy-start | bytes 786436
  129.9 2.5 copy-start.11
  132.1 0.9 copy-start.5
  132.6 1.0 copy-start.4
  133.6 1.0 copy-start.3
  134.1 1.0 copy-start.2
  137.0 4.7 %copy-start.16 = (f32[1,256,256]{2,1,0:T(8,128)S(1)}, f32[1,256,256]{2,1,0:T(8,128)}, u32[]{:S(2)}) copy-start(f32[1,256,256]{2,1,0:T(8,128)} %convolution_bitcast_fusion.8) | copy-start | bytes 786436
  137.0 11.7 %all-to-all-start = ((bf16[1,1,16,32,256]{4,3,1,0,2:T(8,128)(2,1)}), bf16[1,1,16,32,256]{4,3,1,0,2:T(8,128)(2,1)S(1)}, u32[]{:S(2)}, u32[]{:S(2)}) async-start(bf16[1,1,16,32,256]{4,3,1,0,2:T(8,128)(2,1)} %bitcast.267), calls=%async_computation | async-start | bytes 524288 | tf_op jit(solution)/shard_map/all_to_all | solution.py:115
  140.7 87.1 %reduce-scatter.2.cloned.1.call-start = ((), (), s32[]{:S(2)}) async-start(), calls=%async_computation.5 | async-start | bytes 3342336 | tf_op jit(solution)/shard_map/reduce_scatter | solution.py:146
  141.7 1.0 copy-start.14
  141.8 1.0 copy-start.15
  141.8 1.1 copy-start.17
  148.7 0.8 copy-start.9
  151.6 76.2 %copy-start.13 = (bf16[3,256,256]{2,1,0:T(8,128)(2,1)S(1)}, bf16[3,256,256]{2,1,0:T(8,128)(2,1)}, u32[]{:S(2)}) copy-start(bf16[3,256,256]{2,1,0:T(8,128)(2,1)} %param.11) | copy-start | bytes 1179652
  151.6 76.4 %copy-start.10 = (bf16[16,1,32,256]{3,2,0,1:T(8,128)(2,1)S(1)}, bf16[16,1,32,256]{3,2,0,1:T(8,128)(2,1)}, u32[]{:S(2)}) copy-start(bf16[16,1,32,256]{3,2,0,1:T(8,128)(2,1)} %copy-done.9) | copy-start | bytes 786436
  151.7 257.3 %all-gather.3.cloned.1.call-start = ((), (), s32[]{:S(2)}) async-start(), calls=%async_computation.6 | async-start | bytes 6488064 | tf_op jit(solution)/shard_map/all_gather | solution.py:147
Sparse Core Ops, SparseCore 0:
  151.8 75.9 reduce-scatter.1
  230.9 178.0 all-gather.2
